TPU v7x, 512 devices: a whole 4x4x16 slice. The times are simulated.
512 devices in a mesh: blk: 128 (over y, x_lo, z), quad: 4 (over x_hi, core).
Axes of the slice: x: 4 (x_hi: 2, x_lo: 2; x = x_hi * 2 + x_lo), y: 4, z: 16, core: 2. Of those that a mesh axis runs over, the one named last changes fastest.
Arguments:
- positions: float32 [3, 16384], P(None, ('blk', 'quad')), may hold values from 0 to 1
- forces: float32 [3, 16, 16384], P(None, None, ('blk', 'quad')), may hold values from -6 to 6
Outputs:
- velocity: float32 [3, 16, 16384], P(None, None, ('blk', 'quad'))
All inputs are finite; a program needn't handle non-finite values.
Results may differ from a plain program's by a relative error of at most 0.0003.
Values sent between devices are 32-bit elements; how exact they have to be, the bound alone decides.
A program may use at most 64 MiB of HBM per device.

v0:
```python
import math
import jax
import jax.numpy as jnp
from jax import lax
from jax.sharding import PartitionSpec as P

radius_scale = 0.3


def laid_out(tiles, dim):
    lengths = list(tiles.shape[1:])
    lengths[dim] *= tiles.shape[0]
    return jnp.moveaxis(tiles, 0, dim).reshape(lengths)


def copy_for_each(value, axis):
    peers = lax.axis_size(axis)
    return lax.all_to_all(
        jnp.broadcast_to(value[None], (peers, *value.shape)), axis, 0, 0, tiled=True
    )


def gather_directly(value, axis, dim):
    return laid_out(copy_for_each(value, axis), dim)


def gather_turned(arrays, axis, dims):
    turned = [jnp.moveaxis(a, dim, 0) for a, dim in zip(arrays, dims)]
    widths = [t[0].size for t in turned]
    both = jnp.concatenate([t.reshape(-1, w) for t, w in zip(turned, widths)], axis=1)
    whole = lax.all_gather(both, axis, axis=0, tiled=True)
    tiles = jnp.split(whole, [sum(widths[:k]) for k in range(1, len(widths))], axis=1)
    return tuple(
        (
            jnp.moveaxis(b.reshape(-1, *t.shape[1:]), 0, dim)
            for b, t, dim in zip(tiles, turned, dims)
        )
    )


def in_blocks(value, dim, peers):
    before, after = (value.shape[:dim], value.shape[dim + 1 :])
    return jnp.moveaxis(value.reshape(*before, peers, -1, *after), dim, 0)


def sent_and_summed(value, axis, dim):
    peers = lax.axis_size(axis)
    tiles = lax.all_to_all(in_blocks(value, dim, peers), axis, 0, 0, tiled=True)
    return jnp.sum(tiles, axis=0)


def mobility_tile(home_pos, visit_pos, radius):
    separation = home_pos[:, :, None] - visit_pos[:, None, :]
    squared = jnp.sum(separation * separation, axis=0)
    distance = jnp.sqrt(squared)
    far_dist = jnp.maximum(distance, 2.0 * radius)
    inverse = 1.0 / far_dist
    ratio_sq = radius * radius * inverse * inverse
    factor = 0.75 * radius * inverse
    iso_far = factor * (1.0 + 2.0 / 3.0 * ratio_sq)
    dyad_far = factor * (1.0 - 2.0 * ratio_sq) * inverse * inverse
    iso_near = 1.0 - 9.0 / 32.0 * distance / radius
    dyad_near = 3.0 / 32.0 / (radius * jnp.maximum(distance, radius / 1000.0))
    near_mask = distance < 2.0 * radius
    coef_iso = jnp.where(near_mask, iso_near, iso_far)
    coef_dyad = jnp.where(near_mask, dyad_near, dyad_far)
    identity = jnp.eye(3, dtype=jnp.float32)
    return (
        coef_dyad[None, None] * separation[:, None] * separation[None, :]
        + identity[:, :, None, None] * coef_iso[None, None]
    )


def body(positions, forces):
    vectors = forces.shape[1]
    local_rows = positions.shape[1]
    total = local_rows * lax.axis_size("blk") * lax.axis_size("quad")
    radius = radius_scale / total ** (1.0 / 3.0)
    flat_force = forces.reshape(3 * vectors, local_rows)
    block_pos = gather_directly(positions, "quad", 1)
    block_rows = block_pos.shape[1]
    partial_sum = jnp.zeros((3, vectors, block_rows), jnp.float32)
    part_pos, part_force = gather_turned((positions, flat_force), "blk", (1, 1))
    count = part_pos.shape[1]
    width = math.gcd(count, 512)

    def one_block(index, running):
        col_pos = lax.dynamic_slice_in_dim(part_pos, index * width, width, 1)
        col_force = lax.dynamic_slice_in_dim(part_force, index * width, width, 1).reshape(
            3, vectors, width
        )
        kernel = mobility_tile(block_pos, col_pos, radius)
        return running + jnp.einsum(
            "cdij,dvj->cvi", kernel, col_force, precision=lax.Precision.HIGHEST
        )

    partial_sum = lax.fori_loop(0, count // width, one_block, partial_sum)
    velocity = sent_and_summed(partial_sum, "quad", 2)
    return velocity


def solution(mesh):
    in_specs = (P(None, ("blk", "quad")), P(None, None, ("blk", "quad")))
    out_specs = P(None, None, ("blk", "quad"))
    return jax.shard_map(body, mesh=mesh, in_specs=in_specs, out_specs=out_specs, check_vma=False)
```

profile of v0, /device:TPU:1, one launch (start us, length us, event | category | flops | bytes accessed | tf_op | source)
XLA Modules:
  0.0 370.5 jit_solution(10042499356964226688)
XLA Ops:
  0.0 1.3 broadcast_in_dim.28
  1.3 10.1 %all-to-all-start = ((f32[4,3,32]{2,1,0:T(4,128)}), f32[4,3,32]{2,1,0:T(4,128)S(1)}, u32[]{:S(2)}, u32[]{:S(2)}) async-start(f32[4,3,32]{2,1,0:T(4,128)} %broadcast_in_dim.28), calls=%async_computation | async-start | bytes 16384 | tf_op jit(solution)/shard_map/all_to_all | solution.py:18
  11.4 0.7 pad_maximum_fusion
  12.2 262.2 %all_gather.3 = f32[4096,51]{1,0:T(8,128)S(1)} all-gather(f32[32,51]{1,0:T(8,128)S(1)} %copy.8), channel_id=1, replica_groups=mesh['blk'=128,'quad'=4] {'blk'}, dimensions={0}, use_global_device_ids=true | all-gather | bytes 842112 | tf_op jit(solution)/shard_map/all_gather | solution.py:31
  274.4 1.5 slice_bitcast_fusion
  275.9 0.6 slice_bitcast_fusion.1
  276.5 2.2 copy.11
  278.7 0.6 copy.9
  279.5 0.5 copy-done
  280.0 22.7 %while.17 = (s32[]{:T(128)}, f32[3,16,128]{2,1,0:T(8,128)S(1)}, f32[48,4096]{1,0:T(8,128)S(1)}, f32[3,4,32]{2,1,0:T(4,128)}, f32[3,4096]{1,0:T(4,128)S(1)}, /*in...) while((s32[]{:T(128)}, f32[3,16,128]{2,1,0:T(8,128)S(1)}, ...), condition=%wide.wide.region_2.3_spmd.clone, body=%wide.wide.region_0.2_spmd.clone.sunk | while | flops 117321752 | bytes 5090549 | solution.py:97
  280.1 0.3 fusion.29
  280.6 2.2 fusion.31
  283.4 2.2 fusion.31
  286.3 2.2 fusion.31
  289.1 2.2 fusion.31
  291.5 0.3 fusion.29
  291.9 2.2 fusion.31
  294.8 2.2 fusion.31
  297.6 2.2 fusion.31
  300.5 2.2 fusion.31
  302.9 65.6 %all_to_all.10 = f32[4,1,1536]{2,1,0:T(1,128)S(1)} all-to-all(f32[4,1,1536]{2,1,0:T(1,128)S(1)} %reshape.73), channel_id=1, replica_groups=mesh['blk'=128,'quad'=4] {'quad'}, dimensions={0} | all-to-all | bytes 49152 | tf_op jit(solution)/shard_map/all_to_all | solution.py:48
  368.5 0.5 broadcast.294
  369.0 0.7 reduce
  369.8 0.6 reduce_sum.25
  (56 shorter events, 4.7 us)
Async XLA Ops:
  1.3 278.1 %all-to-all-start = ((f32[4,3,32]{2,1,0:T(4,128)}), f32[4,3,32]{2,1,0:T(4,128)S(1)}, u32[]{:S(2)}, u32[]{:S(2)}) async-start(f32[4,3,32]{2,1,0:T(4,128)} %broadcast_in_dim.28), calls=%async_computation | async-start | bytes 16384 | tf_op jit(solution)/shard_map/all_to_all | solution.py:18
  279.4 0.6 copy-start
where the time goes:
time: 371 us; the launch traced here: 370 us
  blocking collectives  328 us (88%)
  matrix products  17.5 us (5%)
  starting transfers between devices  10.1 us (3%)
  local copies, waits for them, and re-layouts  7.87 us (2%)
  other arithmetic  6.63 us (2%)
    all_gather x1, blocking collectives, gather_turned(): whole = lax.all_gather(both, axis, axis=0, tiled=True)  262 us
    all_to_all x1, blocking collectives, sent_and_summed(): tiles = lax.all_to_all(in_blocks(value, dim, peers), axis, 0, 0, tiled=True)  65.6 us
    dot_general x8, matrix products, one_block(): jnp.einsum('cdij,dvj->cvi', kernel, col_force, precision=lax.Precision.HI...  17.5 us
    all_to_all x1, starting transfers between devices, copy_for_each(): lax.all_to_all(jnp.broadcast_to(value[None], (peers, *value.shape)), axis...  10.1 us
  transfers between devices with their start and end apart: 1, of which 0 were waited for; matrix products, arithmetic and copies ran while one was open for 2% of the time, Pallas kernels for 0%

commit v1 on v0

--- a/solution.py
+++ b/solution.py
@@ -28,7 +28,12 @@
     turned = [jnp.moveaxis(a, dim, 0) for a, dim in zip(arrays, dims)]
     widths = [t[0].size for t in turned]
     both = jnp.concatenate([t.reshape(-1, w) for t, w in zip(turned, widths)], axis=1)
-    whole = lax.all_gather(both, axis, axis=0, tiled=True)
+    whole = jnp.concatenate(
+        lax.all_to_all(
+            jnp.stack(lax.axis_size(axis) * [both], 0), axis_name=axis, concat_axis=0, split_axis=0
+        ),
+        0,
+    )
     tiles = jnp.split(whole, [sum(widths[:k]) for k in range(1, len(widths))], axis=1)
     return tuple(
         (

time: 371 us -> 126 us (0.34)
  blocking collectives: 328 us -> 12.8 us
  waiting for transfers between devices: 0.01 us -> 42 us
  starting transfers between devices: 10.1 us -> 25.7 us
  local copies, waits for them, and re-layouts: 7.87 us -> 16.2 us
    all_gather x1 -> x0, blocking collectives: 262 us -> none  [gather_turned(): whole = lax.all_gather(both, axis, axis=0, tiled=True)]
    all_to_all x1, blocking collectives: 65.6 us -> 12.8 us  [sent_and_summed(): tiles = lax.all_to_all(in_blocks(value, dim, peers), axis, 0, 0, tiled=True)]
    all_to_all x0 -> x1, waiting for transfers between devices: none -> 42 us  [gather_turned(): lax.all_to_all(jnp.stack(lax.axis_size(axis) * [both], 0), axis_name=axis...]
    all_to_all x0 -> x1, starting transfers between devices: none -> 15.6 us  [gather_turned(): lax.all_to_all(jnp.stack(lax.axis_size(axis) * [both], 0), axis_name=axis...]
    unnamed x7 -> x11, local copies, waits for them, and re-layouts: 3.5 us -> 10.2 us
  transfers between devices with their start and end apart: 1 -> 2, of which waited for: 0 -> 1; matrix products, arithmetic and copies ran while one was open for 2% -> 4% of each run, Pallas kernels for 0% -> 0%
where the time goes in v1:
time: 126 us; the launch traced here: 124 us
  waiting for transfers between devices  42 us (33%)
  starting transfers between devices  25.7 us (20%)
  matrix products  17.5 us (14%)
  local copies, waits for them, and re-layouts  16.2 us (13%)
  blocking collectives  12.8 us (10%)
  other arithmetic  9.24 us (7%)
    all_to_all x1, waiting for transfers between devices, gather_turned(): lax.all_to_all(jnp.stack(lax.axis_size(axis) * [both], 0), axis_name=axis...  42 us
    dot_general x8, matrix products, one_block(): jnp.einsum('cdij,dvj->cvi', kernel, col_force, precision=lax.Precision.HI...  17.5 us
    all_to_all x1, starting transfers between devices, gather_turned(): lax.all_to_all(jnp.stack(lax.axis_size(axis) * [both], 0), axis_name=axis...  15.6 us
    all_to_all x1, blocking collectives, sent_and_summed(): tiles = lax.all_to_all(in_blocks(value, dim, peers), axis, 0, 0, tiled=True)  12.8 us
    unnamed x11, local copies, waits for them, and re-layouts  10.2 us
    all_to_all x1, starting transfers between devices, copy_for_each(): lax.all_to_all(jnp.broadcast_to(value[None], (peers, *value.shape)), axis...  10.1 us
    transpose x2, local copies, waits for them, and re-layouts, gather_turned(): jnp.moveaxis(b.reshape(-1, *t.shape[1:]), 0, dim)  3.39 us
    all_to_all x1, other arithmetic, gather_turned(): lax.all_to_all(jnp.stack(lax.axis_size(axis) * [both], 0), axis_name=axis...  2.64 us
  transfers between devices with their start and end apart: 2, of which 1 were waited for; matrix products, arithmetic and copies ran while one was open for 4% of the time, Pallas kernels for 0%

profile of v1, /device:TPU:1, one launch (start us, length us, event | category | flops | bytes accessed | tf_op | source)
XLA Modules:
  0.0 124.0 jit_solution(762381580804943291)
XLA Ops:
  0.0 1.3 %broadcast_in_dim.28 = f32[4,3,32]{2,1,0:T(4,128)} broadcast(f32[3,32]{1,0:T(4,128)} %param.4), dimensions={1,2} | broadcast | bytes 1920 | tf_op jit(solution)/shard_map/broadcast_in_dim | solution.py:19
  1.3 10.1 %all-to-all-start.1 = ((f32[4,3,32]{2,1,0:T(4,128)}), f32[4,3,32]{2,1,0:T(4,128)S(1)}, u32[]{:S(2)}, u32[]{:S(2)}) async-start(f32[4,3,32]{2,1,0:T(4,128)} %broadcast_in_dim.28), calls=%async_computation.1 | async-start | bytes 16384 | tf_op jit(solution)/shard_map/all_to_all | solution.py:18
  11.4 0.7 pad_maximum_fusion
  12.5 4.1 %reshape.79 = f32[128,1,1632]{2,1,0:T(1,128)} reshape(f32[128,32,51]{2,1,0:T(8,128)S(1)} %stack.2) | data formatting | bytes 1671168
  16.5 15.6 %all-to-all-start = ((f32[128,1,1632]{2,1,0:T(1,128)}), f32[128,1,1632]{2,1,0:T(1,128)S(1)}, u32[]{:S(2)}, u32[]{:S(2)}) async-start(f32[128,1,1632]{2,1,0:T(1,128)} %reshape.79), calls=%async_computation | async-start | bytes 1703936 | tf_op jit(solution)/shard_map/all_to_all | solution.py:32
  32.3 42.0 %all-to-all-done = f32[128,1,1632]{2,1,0:T(1,128)S(1)} async-done(((f32[128,1,1632]{2,1,0:T(1,128)}), f32[128,1,1632]{2,1,0:T(1,128)S(1)}, u32[]{:S(2)}, u32[]{:S(2)}) %all-to-all-start) | async-done | bytes 835616 | tf_op jit(solution)/shard_map/all_to_all | solution.py:32
  74.8 2.6 %reduce = f32[128,1632]{1,0:T(8,128)S(1)} reduce(f32[128,1,1632]{2,1,0:T(1,128)S(1)} %all-to-all-done, f32[]{:T(128)} %broadcast.296), dimensions={1}, to_apply=%all_to_all.9.reduce_sub_computation | reduce | bytes 1671172 | tf_op jit(solution)/shard_map/all_to_all | solution.py:32
  77.4 3.0 %reshape.80 = f32[128,32,51]{2,1,0:T(8,128)S(1)} reshape(f32[128,1632]{1,0:T(8,128)S(1)} %reduce) | data formatting | bytes 1671168
  80.4 1.4 %slice_bitcast_fusion = f32[3,4096]{0,1:T(8,128)} fusion(f32[4096,51]{1,0:T(8,128)S(1)} %bitcast.31), kind=kLoop, calls=%fused_computation.23 | loop fusion | bytes 98304 | tf_op jit(solution)/shard_map/transpose | solution.py:40
  81.8 2.0 %slice_bitcast_fusion.1 = f32[48,4096]{0,1:T(8,128)} fusion(f32[4096,51]{1,0:T(8,128)S(1)} %bitcast.32), kind=kLoop, calls=%fused_computation.24 | loop fusion | bytes 1572864 | tf_op jit(solution)/shard_map/transpose | solution.py:40
  83.8 2.4 %copy.13 = f32[3,4096]{1,0:T(4,128)S(1)} copy(f32[3,4096]{0,1:T(8,128)} %slice_bitcast_fusion) | data formatting | bytes 98304
  86.2 0.6 copy.11
  86.8 22.8 %while.17 = (s32[]{:T(128)}, f32[3,16,128]{2,1,0:T(8,128)S(1)}, f32[48,4096]{1,0:T(8,128)S(1)}, f32[3,4,32]{2,1,0:T(4,128)}, f32[3,4096]{1,0:T(4,128)S(1)}, /*in...) while((s32[]{:T(128)}, f32[3,16,128]{2,1,0:T(8,128)S(1)}, ...), condition=%wide.wide.region_2.3_spmd.clone, body=%wide.wide.region_0.2_spmd.clone.sunk | while | flops 117321752 | bytes 5090549 | solution.py:102
  87.4 2.2 %fusion.31 = f32[3,16,128]{2,1,0:T(8,128)S(1)} fusion(f32[3,16,512,1]{2,1,0,3:T(8,128)S(1)} %bitcast.33, f32[128,512]{1,0:T(8,128)S(1)} %get-tuple-element.250, f32[3,3]{1,0:T(4,128)S(1)} %fusion.30, f32[3,128,512]{2,1,0:T(8,128)S(1)} %get-tuple-element.252, f32[3,128,512]{2,1,0:T(8,128)S(1)} %get-tuple-element.253, ...), kind=kOutput, calls=%fused_computation.9.clone.clone.1 | convolution fusion | flops 115027968 | bytes 1982501 | tf_op jit(solution)/shard_map/while/body/eval_jaxpr/cdij,dvj->cvi/dot_general | solution.py:98
  90.3 2.2 %fusion.31 = f32[3,16,128]{2,1,0:T(8,128)S(1)} fusion(f32[3,16,512,1]{2,1,0,3:T(8,128)S(1)} %bitcast.33, f32[128,512]{1,0:T(8,128)S(1)} %get-tuple-element.250, f32[3,3]{1,0:T(4,128)S(1)} %fusion.30, f32[3,128,512]{2,1,0:T(8,128)S(1)} %get-tuple-element.252, f32[3,128,512]{2,1,0:T(8,128)S(1)} %get-tuple-element.253, ...), kind=kOutput, calls=%fused_computation.9.clone.clone.1 | convolution fusion | flops 115027968 | bytes 1982501 | tf_op jit(solution)/shard_map/while/body/eval_jaxpr/cdij,dvj->cvi/dot_general | solution.py:98
  93.1 2.2 %fusion.31 = f32[3,16,128]{2,1,0:T(8,128)S(1)} fusion(f32[3,16,512,1]{2,1,0,3:T(8,128)S(1)} %bitcast.33, f32[128,512]{1,0:T(8,128)S(1)} %get-tuple-element.250, f32[3,3]{1,0:T(4,128)S(1)} %fusion.30, f32[3,128,512]{2,1,0:T(8,128)S(1)} %get-tuple-element.252, f32[3,128,512]{2,1,0:T(8,128)S(1)} %get-tuple-element.253, ...), kind=kOutput, calls=%fused_computation.9.clone.clone.1 | convolution fusion | flops 115027968 | bytes 1982501 | tf_op jit(solution)/shard_map/while/body/eval_jaxpr/cdij,dvj->cvi/dot_general | solution.py:98
  96.0 2.2 %fusion.31 = f32[3,16,128]{2,1,0:T(8,128)S(1)} fusion(f32[3,16,512,1]{2,1,0,3:T(8,128)S(1)} %bitcast.33, f32[128,512]{1,0:T(8,128)S(1)} %get-tuple-element.250, f32[3,3]{1,0:T(4,128)S(1)} %fusion.30, f32[3,128,512]{2,1,0:T(8,128)S(1)} %get-tuple-element.252, f32[3,128,512]{2,1,0:T(8,128)S(1)} %get-tuple-element.253, ...), kind=kOutput, calls=%fused_computation.9.clone.clone.1 | convolution fusion | flops 115027968 | bytes 1982501 | tf_op jit(solution)/shard_map/while/body/eval_jaxpr/cdij,dvj->cvi/dot_general | solution.py:98
  98.8 2.2 %fusion.31 = f32[3,16,128]{2,1,0:T(8,128)S(1)} fusion(f32[3,16,512,1]{2,1,0,3:T(8,128)S(1)} %bitcast.33, f32[128,512]{1,0:T(8,128)S(1)} %get-tuple-element.250, f32[3,3]{1,0:T(4,128)S(1)} %fusion.30, f32[3,128,512]{2,1,0:T(8,128)S(1)} %get-tuple-element.252, f32[3,128,512]{2,1,0:T(8,128)S(1)} %get-tuple-element.253, ...), kind=kOutput, calls=%fused_computation.9.clone.clone.1 | convolution fusion | flops 115027968 | bytes 1982501 | tf_op jit(solution)/shard_map/while/body/eval_jaxpr/cdij,dvj->cvi/dot_general | solution.py:98
  101.7 2.2 %fusion.31 = f32[3,16,128]{2,1,0:T(8,128)S(1)} fusion(f32[3,16,512,1]{2,1,0,3:T(8,128)S(1)} %bitcast.33, f32[128,512]{1,0:T(8,128)S(1)} %get-tuple-element.250, f32[3,3]{1,0:T(4,128)S(1)} %fusion.30, f32[3,128,512]{2,1,0:T(8,128)S(1)} %get-tuple-element.252, f32[3,128,512]{2,1,0:T(8,128)S(1)} %get-tuple-element.253, ...), kind=kOutput, calls=%fused_computation.9.clone.clone.1 | convolution fusion | flops 115027968 | bytes 1982501 | tf_op jit(solution)/shard_map/while/body/eval_jaxpr/cdij,dvj->cvi/dot_general | solution.py:98
  104.5 2.2 %fusion.31 = f32[3,16,128]{2,1,0:T(8,128)S(1)} fusion(f32[3,16,512,1]{2,1,0,3:T(8,128)S(1)} %bitcast.33, f32[128,512]{1,0:T(8,128)S(1)} %get-tuple-element.250, f32[3,3]{1,0:T(4,128)S(1)} %fusion.30, f32[3,128,512]{2,1,0:T(8,128)S(1)} %get-tuple-element.252, f32[3,128,512]{2,1,0:T(8,128)S(1)} %get-tuple-element.253, ...), kind=kOutput, calls=%fused_computation.9.clone.clone.1 | convolution fusion | flops 115027968 | bytes 1982501 | tf_op jit(solution)/shard_map/while/body/eval_jaxpr/cdij,dvj->cvi/dot_general | solution.py:98
  107.3 2.2 %fusion.31 = f32[3,16,128]{2,1,0:T(8,128)S(1)} fusion(f32[3,16,512,1]{2,1,0,3:T(8,128)S(1)} %bitcast.33, f32[128,512]{1,0:T(8,128)S(1)} %get-tuple-element.250, f32[3,3]{1,0:T(4,128)S(1)} %fusion.30, f32[3,128,512]{2,1,0:T(8,128)S(1)} %get-tuple-element.252, f32[3,128,512]{2,1,0:T(8,128)S(1)} %get-tuple-element.253, ...), kind=kOutput, calls=%fused_computation.9.clone.clone.1 | convolution fusion | flops 115027968 | bytes 1982501 | tf_op jit(solution)/shard_map/while/body/eval_jaxpr/cdij,dvj->cvi/dot_general | solution.py:98
  109.8 12.8 %all_to_all.15 = f32[4,1,1536]{2,1,0:T(1,128)S(1)} all-to-all(f32[4,1,1536]{2,1,0:T(1,128)S(1)} %reshape.81), channel_id=1, replica_groups=mesh['blk'=128,'quad'=4] {'quad'}, dimensions={0} | all-to-all | bytes 49152 | tf_op jit(solution)/shard_map/all_to_all | solution.py:53
  122.6 0.7 reduce.1
  123.4 0.6 reduce_sum.25
  (63 shorter events, 6.0 us)
Async XLA Ops:
  1.3 15.3 %all-to-all-start.1 = ((f32[4,3,32]{2,1,0:T(4,128)}), f32[4,3,32]{2,1,0:T(4,128)S(1)}, u32[]{:S(2)}, u32[]{:S(2)}) async-start(f32[4,3,32]{2,1,0:T(4,128)} %broadcast_in_dim.28), calls=%async_computation.1 | async-start | bytes 16384 | tf_op jit(solution)/shard_map/all_to_all | solution.py:18
  16.5 57.7 %all-to-all-start = ((f32[128,1,1632]{2,1,0:T(1,128)}), f32[128,1,1632]{2,1,0:T(1,128)S(1)}, u32[]{:S(2)}, u32[]{:S(2)}) async-start(f32[128,1,1632]{2,1,0:T(1,128)} %reshape.79), calls=%async_computation | async-start | bytes 1703936 | tf_op jit(solution)/shard_map/all_to_all | solution.py:32
  32.2 48.3 %copy-start.1 = (f32[3,4,32]{2,1,0:T(4,128)}, f32[3,4,32]{2,1,0:T(4,128)S(1)}, u32[]{:S(2)}) copy-start(f32[3,4,32]{2,1,0:T(4,128)S(1)} %copy.12) | copy-start | bytes 4612
  83.8 2.4 %copy-start = (f32[48,4096]{0,1:T(8,128)S(1)}, f32[48,4096]{0,1:T(8,128)}, u32[]{:S(2)}) copy-start(f32[48,4096]{0,1:T(8,128)} %slice_bitcast_fusion.1) | copy-start | bytes 2359300
